TPU v7x, 32 devices: a whole 2x2x4 slice. The times are simulated.
32 devices in a mesh: dp: 8 (over y, x, core), shard: 4 (over z).
Axes of the slice: x: 2, y: 2, z: 4, core: 2. Of those that a mesh axis runs over, the one named last changes fastest.
Arguments:
- tokens: bfloat16 [49152, 576], P(('dp', 'shard')), may hold values from -6 to 6
- segments: int32 [49152], P(('dp', 'shard')), may hold values from 0 to 7, as said below
- norm_attn: bfloat16 [576], P('shard'), may hold values from 0.5 to 1.5
- w_query: bfloat16 [576, 576], P('shard'), may hold values from -0.25 to 0.25
- w_key: bfloat16 [576, 192], P('shard'), may hold values from -0.25 to 0.25
- w_value: bfloat16 [576, 192], P('shard'), may hold values from -0.25 to 0.25
- w_out: bfloat16 [576, 576], P('shard'), may hold values from -1 to 1
- norm_ffn: bfloat16 [576], P('shard'), may hold values from 0.5 to 1.5
- w_gate: bfloat16 [576, 1536], P('shard'), may hold values from -0.25 to 0.25
- w_up: bfloat16 [576, 1536], P('shard'), may hold values from -0.25 to 0.25
- w_down: bfloat16 [1536, 576], P('shard'), may hold values from -0.15625 to 0.15625
- cotangent: bfloat16 [49152, 576], P(('dp', 'shard')), may hold values from -6 to 6
Outputs:
- output: bfloat16 [49152, 576], P(('dp', 'shard'))
- input_grad: bfloat16 [49152, 576], P(('dp', 'shard'))
- grad_norm_attn: float32 [576], P('shard')
- grad_query: float32 [576, 576], P('shard')
- grad_key: float32 [576, 192], P('shard')
- grad_value: float32 [576, 192], P('shard')
- grad_out: float32 [576, 576], P('shard')
- grad_norm_ffn: float32 [576], P('shard')
- grad_gate: float32 [576, 1536], P('shard')
- grad_up: float32 [576, 1536], P('shard')
- grad_down: float32 [1536, 576], P('shard')
Inputs may be any that keep to these rules, and one draw needn't show every extreme that they name: `segments`: within each aligned block of 512 tokens the segment ids begin at 0 and never fall; every fourth block is one sequence of 512 tokens.
All inputs are finite; a program needn't handle non-finite values.
Results may differ from a plain program's by a relative error of at most 0.012.
Values may be sent and summed in bfloat16 or wider, within the bound.
A program may use at most 192 MiB of HBM per device.

v0:
```python
import jax
import jax.numpy as jnp
from jax import lax
from jax.sharding import PartitionSpec as P

HQ = 9
KVH = 3
HD = 64
BLOCK = 512


epsilon = 1e-05


def matmul(former, latter):
    return jnp.dot(former, latter, preferred_element_type=jnp.float32)


def contract_rows(former, latter):
    return lax.dot_general(
        former, latter, (((0,), (0,)), ((), ())), preferred_element_type=jnp.float32
    )


def times_transposed(former, latter):
    return lax.dot_general(
        former, latter, (((1,), (1,)), ((), ())), preferred_element_type=jnp.float32
    )


def places_of(segment_ids):
    slot_index = jnp.arange(BLOCK, dtype=jnp.int32)
    earlier = jnp.concatenate([segment_ids[:, :1] - 1, segment_ids[:, :-1]], axis=1)
    starts = jnp.where(segment_ids != earlier, slot_index[None, :], 0)
    return (slot_index[None, :] - lax.cummax(starts, axis=1)).astype(jnp.float32)


def rope_tables(places):
    frequency = 100000.0 ** (jnp.arange(HD // 2, dtype=jnp.float32) * (-2.0 / HD))
    angles = places[..., None] * frequency
    angles = jnp.concatenate([angles, angles], axis=-1)
    return (jnp.cos(angles)[..., None, :], jnp.sin(angles)[..., None, :])


def rotate(values, cosine, sine_table):
    half_size = values.shape[-1] // 2
    turned = jnp.concatenate([-values[..., half_size:], values[..., :half_size]], axis=-1)
    return values * cosine + turned * sine_table


def unrotate(gradient, cosine, sine_table):
    half_size = gradient.shape[-1] // 2
    scaled = gradient * sine_table
    moved_back = jnp.concatenate([scaled[..., half_size:], -scaled[..., :half_size]], axis=-1)
    return gradient * cosine + moved_back


def norm_back(gradient, inputs, inverse, scales):
    weighted = gradient * scales
    input_part = inverse * (
        weighted - inputs * inverse * inverse * jnp.mean(weighted * inputs, axis=-1, keepdims=True)
    )
    scale_part = jnp.sum(gradient * inputs * inverse, axis=0)
    return (input_part, scale_part)


def masked_scores(queries, keys_rot, allowed):
    scores = jnp.einsum(
        "qkgd,pkd->kgqp", queries, keys_rot, preferred_element_type=jnp.float32
    ) * HD ** (-0.5)
    return jnp.where(allowed, scores, -1e30)


def attend_block(operands):
    queries, keys_rot, values, allowed = operands
    scores = masked_scores(queries, keys_rot, allowed)
    highest = jnp.max(scores, axis=-1, keepdims=True)
    exponents = jnp.exp(scores - highest)
    totals = jnp.sum(exponents, axis=-1, keepdims=True)
    weights = (exponents / totals).astype(jnp.bfloat16)
    mixed_heads = jnp.einsum("kgqp,pkd->qkgd", weights, values, preferred_element_type=jnp.float32)
    return (mixed_heads, highest + jnp.log(totals))


def attend_back(operands):
    queries, keys_rot, values, allowed, log_totals, mixed_grad = operands
    scores = masked_scores(queries, keys_rot, allowed)
    probs_all = jnp.exp(scores - log_totals)
    probs_grad = jnp.einsum(
        "qkgd,pkd->kgqp", mixed_grad, values, preferred_element_type=jnp.float32
    )
    score_grad = (
        probs_all * (probs_grad - jnp.sum(probs_all * probs_grad, axis=-1, keepdims=True))
    ).astype(jnp.bfloat16)
    value_grad = jnp.einsum(
        "kgqp,qkgd->pkd",
        probs_all.astype(jnp.bfloat16),
        mixed_grad,
        preferred_element_type=jnp.float32,
    )
    query_grad = jnp.einsum(
        "kgqp,pkd->qkgd", score_grad, keys_rot, preferred_element_type=jnp.float32
    ) * HD ** (-0.5)
    key_grad = jnp.einsum(
        "kgqp,qkgd->pkd", score_grad, queries, preferred_element_type=jnp.float32
    ) * HD ** (-0.5)
    return (query_grad, key_grad, value_grad)


def shards(
    tokens,
    segments,
    norm_attn,
    w_query,
    w_key,
    w_value,
    w_out,
    norm_ffn,
    w_gate,
    w_up,
    w_down,
    cotangent,
):
    gathered = (
        lax.all_gather(norm_attn, "shard", axis=0, tiled=True),
        lax.all_gather(w_query, "shard", axis=0, tiled=True),
        lax.all_gather(w_key, "shard", axis=0, tiled=True),
        lax.all_gather(w_value, "shard", axis=0, tiled=True),
        lax.all_gather(w_out, "shard", axis=0, tiled=True),
        lax.all_gather(norm_ffn, "shard", axis=0, tiled=True),
        lax.all_gather(w_gate, "shard", axis=0, tiled=True),
        lax.all_gather(w_up, "shard", axis=0, tiled=True),
        lax.all_gather(w_down, "shard", axis=0, tiled=True),
    )
    gain_one, query_w, key_w, value_w, out_w, gain_two, gate_w, up_w, down_w = gathered
    row_count = tokens.shape[0]
    model_width = tokens.shape[1]
    blocks = row_count // BLOCK
    groups = HQ // KVH
    inputs = tokens.astype(jnp.float32)
    segment_ids = segments.reshape(blocks, BLOCK)
    cosine, sine_table = rope_tables(places_of(segment_ids))
    cosine = cosine.reshape(row_count, 1, HD)
    sine_table = sine_table.reshape(row_count, 1, HD)
    slot_index = jnp.arange(BLOCK, dtype=jnp.int32)
    allowed = (segment_ids[:, :, None] == segment_ids[:, None, :]) & (
        slot_index[:, None] >= slot_index[None, :]
    )
    allowed = allowed[:, None, None]
    inverse_one = lax.rsqrt(jnp.mean(inputs * inputs, axis=-1, keepdims=True) + epsilon)
    normed_one = (inputs * inverse_one * gain_one.astype(jnp.float32)).astype(jnp.bfloat16)
    queries = rotate(
        matmul(normed_one, query_w).reshape(row_count, HQ, HD), cosine, sine_table
    ).astype(jnp.bfloat16)
    keys_rot = rotate(
        matmul(normed_one, key_w).reshape(row_count, KVH, HD), cosine, sine_table
    ).astype(jnp.bfloat16)
    values = matmul(normed_one, value_w).astype(jnp.bfloat16)
    query_blocks = queries.reshape(blocks, BLOCK, KVH, groups, HD)
    key_blocks = keys_rot.reshape(blocks, BLOCK, KVH, HD)
    value_blocks = values.reshape(blocks, BLOCK, KVH, HD)
    mixed_heads, log_totals = lax.map(
        attend_block, (query_blocks, key_blocks, value_blocks, allowed)
    )
    mixed_heads = mixed_heads.reshape(row_count, model_width).astype(jnp.bfloat16)
    middle = inputs + matmul(mixed_heads, out_w)
    inverse_two = lax.rsqrt(jnp.mean(middle * middle, axis=-1, keepdims=True) + epsilon)
    normed_two = (middle * inverse_two * gain_two.astype(jnp.float32)).astype(jnp.bfloat16)
    gate_values = matmul(normed_two, gate_w)
    upward = matmul(normed_two, up_w)
    sigmoid_gate = jax.nn.sigmoid(gate_values)
    silu_gate = gate_values * sigmoid_gate
    hidden = (silu_gate * upward).astype(jnp.bfloat16)
    output = (middle + matmul(hidden, down_w)).astype(jnp.bfloat16)
    regathered = (
        lax.all_gather(norm_attn, "shard", axis=0, tiled=True),
        lax.all_gather(w_query, "shard", axis=0, tiled=True),
        lax.all_gather(w_key, "shard", axis=0, tiled=True),
        lax.all_gather(w_value, "shard", axis=0, tiled=True),
        lax.all_gather(w_out, "shard", axis=0, tiled=True),
        lax.all_gather(norm_ffn, "shard", axis=0, tiled=True),
        lax.all_gather(w_gate, "shard", axis=0, tiled=True),
        lax.all_gather(w_up, "shard", axis=0, tiled=True),
        lax.all_gather(w_down, "shard", axis=0, tiled=True),
    )
    gain_one, query_w, key_w, value_w, out_w, gain_two, gate_w, up_w, down_w = regathered
    down_grad = contract_rows(hidden, cotangent)
    hidden_grad = times_transposed(cotangent, down_w)
    gate_grad = (
        hidden_grad * upward * sigmoid_gate * (1.0 + gate_values * (1.0 - sigmoid_gate))
    ).astype(jnp.bfloat16)
    upward_grad = (hidden_grad * silu_gate).astype(jnp.bfloat16)
    gate_w_grad = contract_rows(normed_two, gate_grad)
    up_w_grad = contract_rows(normed_two, upward_grad)
    normed_two_grad = times_transposed(gate_grad, gate_w) + times_transposed(upward_grad, up_w)
    middle_part, gain_two_grad = norm_back(
        normed_two_grad, middle, inverse_two, gain_two.astype(jnp.float32)
    )
    middle_grad = cotangent.astype(jnp.float32) + middle_part
    branch_grad = middle_grad.astype(jnp.bfloat16)
    out_w_grad = contract_rows(mixed_heads, branch_grad)
    mixed_grad = (
        times_transposed(branch_grad, out_w)
        .astype(jnp.bfloat16)
        .reshape(blocks, BLOCK, KVH, groups, HD)
    )
    query_grad, key_grad, value_grad = lax.map(
        attend_back, (query_blocks, key_blocks, value_blocks, allowed, log_totals, mixed_grad)
    )
    query_grad = (
        unrotate(query_grad.reshape(row_count, HQ, HD), cosine, sine_table)
        .reshape(row_count, model_width)
        .astype(jnp.bfloat16)
    )
    key_grad = (
        unrotate(key_grad.reshape(row_count, KVH, HD), cosine, sine_table)
        .reshape(row_count, KVH * HD)
        .astype(jnp.bfloat16)
    )
    value_grad = value_grad.reshape(row_count, KVH * HD).astype(jnp.bfloat16)
    query_w_grad = contract_rows(normed_one, query_grad)
    key_w_grad = contract_rows(normed_one, key_grad)
    value_w_grad = contract_rows(normed_one, value_grad)
    normed_one_grad = (
        times_transposed(query_grad, query_w)
        + times_transposed(key_grad, key_w)
        + times_transposed(value_grad, value_w)
    )
    input_part, gain_one_grad = norm_back(
        normed_one_grad, inputs, inverse_one, gain_one.astype(jnp.float32)
    )
    input_grad = (middle_grad + input_part).astype(jnp.bfloat16)
    owned_grads = (
        lax.psum_scatter(gain_one_grad, "shard", scatter_dimension=0, tiled=True),
        lax.psum_scatter(query_w_grad, "shard", scatter_dimension=0, tiled=True),
        lax.psum_scatter(key_w_grad, "shard", scatter_dimension=0, tiled=True),
        lax.psum_scatter(value_w_grad, "shard", scatter_dimension=0, tiled=True),
        lax.psum_scatter(out_w_grad, "shard", scatter_dimension=0, tiled=True),
        lax.psum_scatter(gain_two_grad, "shard", scatter_dimension=0, tiled=True),
        lax.psum_scatter(gate_w_grad, "shard", scatter_dimension=0, tiled=True),
        lax.psum_scatter(up_w_grad, "shard", scatter_dimension=0, tiled=True),
        lax.psum_scatter(down_grad, "shard", scatter_dimension=0, tiled=True),
    )
    summed = lax.psum(
        (
            owned_grads[0],
            owned_grads[1],
            owned_grads[2],
            owned_grads[3],
            owned_grads[4],
            owned_grads[5],
            owned_grads[6],
            owned_grads[7],
            owned_grads[8],
        ),
        "dp",
    )
    return (
        output,
        input_grad,
        summed[0],
        summed[1],
        summed[2],
        summed[3],
        summed[4],
        summed[5],
        summed[6],
        summed[7],
        summed[8],
    )


def solution(mesh):
    in_specs = (
        P(("dp", "shard"), None),
        P(("dp", "shard")),
        P("shard"),
        P("shard", None),
        P("shard", None),
        P("shard", None),
        P("shard", None),
        P("shard"),
        P("shard", None),
        P("shard", None),
        P("shard", None),
        P(("dp", "shard"), None),
    )
    out_specs = (
        P(("dp", "shard"), None),
        P(("dp", "shard"), None),
        P("shard"),
        P("shard", None),
        P("shard", None),
        P("shard", None),
        P("shard", None),
        P("shard"),
        P("shard", None),
        P("shard", None),
        P("shard", None),
    )
    return jax.shard_map(shards, mesh=mesh, in_specs=in_specs, out_specs=out_specs, check_vma=False)
```

profile of v0, /device:TPU:0, one launch (start us, length us, event | category | flops | bytes accessed | tf_op | source)
XLA Modules:
  0.0 885.7 jit_solution(16061555991305422175)
XLA Ops:
  16.8 14.4 %all-reduce.7 = (bf16[576]{0:T(1024)(128)(2,1)S(1)}, bf16[576]{0:T(1024)(128)(2,1)}) all-reduce(bf16[576]{0:T(1024)(128)(2,1)S(1)} %dynamic-update-slice, bf16[576]{0:T(1024)(128)(2,1)S(1)} %dynamic-update-slice.1), channel_id=1, replica_groups=mesh['dp'=8,'shard'=4] {'shard'}, use_global_device_ids=true, to_apply=%add | all-reduce | flops 1152 | bytes 4608
  33.1 16.3 %all_gather.38 = bf16[576,192]{1,0:T(8,128)(2,1)S(1)} all-gather(bf16[144,192]{1,0:T(8,128)(2,1)S(1)} %copy-done.33), channel_id=1, replica_groups=mesh['dp'=8,'shard'=4] {'shard'}, dimensions={0}, use_global_device_ids=true | all-gather | bytes 276480 | tf_op jit(solution)/shard_map/all_gather | solution.py:127
  49.5 15.8 %all_gather.37 = bf16[576,192]{1,0:T(8,128)(2,1)S(1)} all-gather(bf16[144,192]{1,0:T(8,128)(2,1)S(1)} %copy-done.34), channel_id=1, replica_groups=mesh['dp'=8,'shard'=4] {'shard'}, dimensions={0}, use_global_device_ids=true | all-gather | bytes 276480 | tf_op jit(solution)/shard_map/all_gather | solution.py:128
  70.8 26.7 %all_gather.39 = bf16[576,576]{1,0:T(8,128)(2,1)} all-gather(bf16[144,576]{1,0:T(8,128)(2,1)S(1)} %copy-done.31), channel_id=1, replica_groups=mesh['dp'=8,'shard'=4] {'shard'}, dimensions={0}, use_global_device_ids=true | all-gather | bytes 829440 | tf_op jit(solution)/shard_map/all_gather | solution.py:126
  97.5 25.3 %all_gather.40 = bf16[576,576]{1,0:T(8,128)(2,1)} all-gather(bf16[144,576]{1,0:T(8,128)(2,1)S(1)} %copy-done.32), channel_id=1, replica_groups=mesh['dp'=8,'shard'=4] {'shard'}, dimensions={0}, use_global_device_ids=true | all-gather | bytes 829440 | tf_op jit(solution)/shard_map/all_gather | solution.py:129
  122.8 4.5 fusion.80
  141.6 3.5 fusion.90
  145.0 6.6 reshape.245
  151.7 3.6 slice_negate_fusion.1
  155.3 4.2 concatenate.52
  159.5 2.7 concatenate.53
  162.1 4.9 fusion.59
  167.5 31.7 %while.26 = (s32[]{:T(128)}, bf16[3,512,3,3,64]{1,4,3,2,0:T(8,128)(2,1)}, f32[3,3,3,512,1]{3,2,1,4,0:T(4,128)}, bf16[3,512,3,64]{1,3,2,0:T(8,128)(2,1)}, pred[3,...) while((s32[]{:T(128)}, ...), condition=%wide.region_6.7_spmd, body=%wide.region_3.6_spmd.sunk | while | flops 632286720 | bytes 46108828 | solution.py:162
  169.0 2.5 fusion.162
  173.5 3.7 fusion.164
  183.9 3.7 fusion.164
  194.3 3.7 fusion.164
  199.2 3.1 copy.56
  203.6 3.4 multiply_reduce_fusion.2
  213.1 8.3 fusion.99
  221.4 7.9 fusion.98
  229.3 14.9 %multiply_convert_fusion = (bf16[1536,1536]{1,0:T(8,128)(2,1)S(1)}, bf16[1536,1536]{1,0:T(8,128)(2,1)S(1)}, bf16[1536,1536]{1,0:T(8,128)(2,1)}) fusion(f32[1536,1536]{1,0:T(8,128)} %fusion.98, f32[1536,1536]{1,0:T(8,128)} %fusion.99, bf16[1536,576]{0,1:T(8,128)(2,1)} %param.27, bf16[1536,576]{0,1:T(8,128)(2,1)} %all-gather.8.cloned.1.call-done), kind=kOutput, calls=%fused_computation.64 | convolution fusion | flops 2753298432 | bytes 36569088 | tf_op jit(solution)/shard_map/dot_general | solution.py:26
  244.3 2.9 fusion.100
  250.1 4.0 multiply_reduce_fusion
  258.5 3.3 reshape.247
  261.8 3.3 copy.60
  265.1 195.4 %while.27 = (s32[]{:T(128)}, f32[3,512,3,3,64]{1,0,4,3,2:T(4,128)}, f32[3,512,3,64]{1,0,3,2:T(4,128)}, bf16[3,512,3,64]{1,3,2,0:T(8,128)(2,1)}, bf16[3,512,3,64]...) while((s32[]{:T(128)}, f32[3,512,3,3,64]{1,0,4,3,2:T(4,128)}, ...), condition=%wide.region_11.12_spmd, body=%wide.region_9.11_spmd.sunk | while | flops 1545727488 | bytes 147141856 | solution.py:207
  269.4 3.8 fusion.178
  273.2 6.1 fusion.174
  279.3 11.2 %fusion.175 = bf16[3,3,512,512]{2,3,1,0:T(8,128)(2,1)} fusion(f32[3,512,512,3]{2,1,3,0:T(8,128)} %get-tuple-element.345, f32[3,512,512,3]{2,1,3,0:T(8,128)} %copy-done, f32[3,3,512]{2,1,0:T(4,128)S(1)} %get-tuple-element.346, f32[3,3,512]{2,1,0:T(4,128)S(1)} %dynamic-slice_bitcast_fusion.7, pred[512,512]{0,1:T(8,128)(4,1)S(1)} %dynamic-slice_bitcast_fusion.8), kind=kLoop, calls=%fused_computation.25.clone.1 | loop fusion | flops 14155776 | bytes 23891968 | tf_op jit(solution)/shard_map/while/body/eval_jaxpr/convert_element_type | solution.py:94
  290.5 4.0 fusion.177
  298.1 8.6 dynamic_update_slice.30
  306.7 23.5 %dynamic_update_slice.29 = f32[3,512,3,3,64]{1,0,4,3,2:T(4,128)} dynamic-update-slice(f32[3,512,3,3,64]{1,0,4,3,2:T(4,128)} %get-tuple-element.384, f32[1,512,3,3,64]{1,0,4,3,2:T(1,128)S(1)} %copy.96, s32[]{:T(128)S(6)} %copy.118, s32[]{:T(128)} %constant.67.clone.1..sunk, s32[]{:T(128)} %constant.67.clone.1..sunk, s32[]{:T(128)} %constant.67.clone.1..sunk, s32[]{:T(128)} %constant.67.clone.1..sunk) | dynamic-update-slice | bytes 2359300 | tf_op jit(solution)/shard_map/while/body/jit(dynamic_update_index_in_dim)/dynamic_update_slice | solution.py:162
  334.4 3.8 fusion.178
  338.2 6.1 fusion.174
  344.3 11.2 %fusion.175 = bf16[3,3,512,512]{2,3,1,0:T(8,128)(2,1)} fusion(f32[3,512,512,3]{2,1,3,0:T(8,128)} %get-tuple-element.345, f32[3,512,512,3]{2,1,3,0:T(8,128)} %copy-done, f32[3,3,512]{2,1,0:T(4,128)S(1)} %get-tuple-element.346, f32[3,3,512]{2,1,0:T(4,128)S(1)} %dynamic-slice_bitcast_fusion.7, pred[512,512]{0,1:T(8,128)(4,1)S(1)} %dynamic-slice_bitcast_fusion.8), kind=kLoop, calls=%fused_computation.25.clone.1 | loop fusion | flops 14155776 | bytes 23891968 | tf_op jit(solution)/shard_map/while/body/eval_jaxpr/convert_element_type | solution.py:94
  355.5 4.0 fusion.177
  363.1 8.6 dynamic_update_slice.30
  371.7 23.5 %dynamic_update_slice.29 = f32[3,512,3,3,64]{1,0,4,3,2:T(4,128)} dynamic-update-slice(f32[3,512,3,3,64]{1,0,4,3,2:T(4,128)} %get-tuple-element.384, f32[1,512,3,3,64]{1,0,4,3,2:T(1,128)S(1)} %copy.96, s32[]{:T(128)S(6)} %copy.118, s32[]{:T(128)} %constant.67.clone.1..sunk, s32[]{:T(128)} %constant.67.clone.1..sunk, s32[]{:T(128)} %constant.67.clone.1..sunk, s32[]{:T(128)} %constant.67.clone.1..sunk) | dynamic-update-slice | bytes 2359300 | tf_op jit(solution)/shard_map/while/body/jit(dynamic_update_index_in_dim)/dynamic_update_slice | solution.py:162
  399.4 3.8 fusion.178
  403.1 6.1 fusion.174
  409.3 11.2 %fusion.175 = bf16[3,3,512,512]{2,3,1,0:T(8,128)(2,1)} fusion(f32[3,512,512,3]{2,1,3,0:T(8,128)} %get-tuple-element.345, f32[3,512,512,3]{2,1,3,0:T(8,128)} %copy-done, f32[3,3,512]{2,1,0:T(4,128)S(1)} %get-tuple-element.346, f32[3,3,512]{2,1,0:T(4,128)S(1)} %dynamic-slice_bitcast_fusion.7, pred[512,512]{0,1:T(8,128)(4,1)S(1)} %dynamic-slice_bitcast_fusion.8), kind=kLoop, calls=%fused_computation.25.clone.1 | loop fusion | flops 14155776 | bytes 23891968 | tf_op jit(solution)/shard_map/while/body/eval_jaxpr/convert_element_type | solution.py:94
  420.5 4.0 fusion.177
  428.0 8.6 dynamic_update_slice.30
  436.7 23.5 %dynamic_update_slice.29 = f32[3,512,3,3,64]{1,0,4,3,2:T(4,128)} dynamic-update-slice(f32[3,512,3,3,64]{1,0,4,3,2:T(4,128)} %get-tuple-element.384, f32[1,512,3,3,64]{1,0,4,3,2:T(1,128)S(1)} %copy.96, s32[]{:T(128)S(6)} %copy.118, s32[]{:T(128)} %constant.67.clone.1..sunk, s32[]{:T(128)} %constant.67.clone.1..sunk, s32[]{:T(128)} %constant.67.clone.1..sunk, s32[]{:T(128)} %constant.67.clone.1..sunk) | dynamic-update-slice | bytes 2359300 | tf_op jit(solution)/shard_map/while/body/jit(dynamic_update_index_in_dim)/dynamic_update_slice | solution.py:162
  463.1 3.0 fusion.84
  470.8 5.3 fusion.76
  476.1 6.7 reshape.249
  482.9 4.2 copy.88
  490.3 2.7 fusion.88
  493.0 7.7 fusion.105
  500.9 7.6 fusion.101
  508.6 7.6 fusion.102
  520.5 3.2 fusion.71
  523.6 21.3 %reduce-scatter.14.cloned.1.call-done = f32[144,576]{1,0:T(8,128)} async-done(((f32[576,576]{1,0:T(8,128)}), f32[144,576]{1,0:T(8,128)}) %reduce-scatter.14.cloned.1.call-update) | async-done | bytes 331792 | tf_op jit(solution)/shard_map/reduce_scatter | solution.py:238
  544.9 35.7 %reduce-scatter.8.cloned.1.call-done = f32[144,576]{1,0:T(8,128)} async-done(((f32[576,576]{1,0:T(8,128)}), f32[144,576]{1,0:T(8,128)}) %reduce-scatter.8.cloned.1.call-update) | async-done | bytes 331792 | tf_op jit(solution)/shard_map/reduce_scatter | solution.py:235
  580.7 67.6 %reduce-scatter.20.cloned.1.call-done = f32[384,576]{0,1:T(8,128)} async-done(((f32[1536,576]{0,1:T(8,128)}), f32[384,576]{0,1:T(8,128)}) %reduce-scatter.20.cloned.1.call-update) | async-done | bytes 884752 | tf_op jit(solution)/shard_map/reduce_scatter | solution.py:242
  648.3 69.0 %reduce-scatter.16.cloned.1.call-done = f32[144,1536]{1,0:T(8,128)} async-done(((f32[576,1536]{1,0:T(8,128)}), f32[144,1536]{1,0:T(8,128)}) %reduce-scatter.16.cloned.1.call-update) | async-done | bytes 884752 | tf_op jit(solution)/shard_map/reduce_scatter | solution.py:240
  717.3 68.8 %reduce-scatter.18.cloned.1.call-done = f32[144,1536]{1,0:T(8,128)} async-done(((f32[576,1536]{1,0:T(8,128)}), f32[144,1536]{1,0:T(8,128)}) %reduce-scatter.18.cloned.1.call-update) | async-done | bytes 884752 | tf_op jit(solution)/shard_map/reduce_scatter | solution.py:241
  786.2 10.9 %all-reduce.6 = (f32[576]{0:T(1024)S(1)}, f32[576]{0:T(1024)S(1)}) all-reduce(f32[576]{0:T(1024)S(1)} %get-tuple-element.161, f32[576]{0:T(1024)S(1)} %copy-done.39), channel_id=2, replica_groups=mesh['dp'=8,'shard'=4] {'shard'}, use_global_device_ids=true, to_apply=%region_14.15.clone | all-reduce | flops 1152 | bytes 9216
  797.2 13.1 %all-reduce.4 = (f32[144]{0:T(256)}, f32[144]{0:T(256)}) all-reduce(f32[144]{0:T(256)S(1)} %dynamic-slice.3, f32[144]{0:T(256)S(1)} %dynamic-slice.5), channel_id=1, replica_groups=mesh['dp'=8,'shard'=4] {'dp'}, use_global_device_ids=true, to_apply=%region_15.16 | all-reduce | flops 288 | bytes 2304 | tf_op jit(solution)/shard_map/psum | solution.py:244
  810.3 5.7 fusion.67
  816.0 6.4 add_convert_fusion
  822.5 45.8 %all-reduce.10.cloned.1.call-done = (f32[144,576]{1,0:T(8,128)}, f32[144,192]{1,0:T(8,128)}, f32[144,192]{1,0:T(8,128)}, f32[144,576]{1,0:T(8,128)}, f32[144,153...) async-done(((f32[144,576]{1,0:T(8,128)}, f32[144,192]{1,0:T(8,128)}, f32[144,192]{1,0:T(8,128)}, f32[144,576]{1,0:T(8,128)}, f32[144,1536]{1,0:T(8,128)}, ...) | async-done | bytes 3538960 | tf_op jit(solution)/shard_map/psum | solution.py:244
  (249 shorter events, 111.1 us)
Async XLA Ops:
  7.2 59.6 %copy-start.2 = (bf16[1536,576]{0,1:T(8,128)(2,1)S(1)}, bf16[1536,576]{0,1:T(8,128)(2,1)}, u32[]{:S(2)}) copy-start(bf16[1536,576]{0,1:T(8,128)(2,1)} %param.16) | copy-start | bytes 5308420
  7.2 25.9 %copy-start.33 = (bf16[144,192]{1,0:T(8,128)(2,1)S(1)}, bf16[144,192]{1,0:T(8,128)(2,1)}, u32[]{:S(2)}) copy-start(bf16[144,192]{1,0:T(8,128)(2,1)} %param.20) | copy-start | bytes 165892
  7.2 42.3 %copy-start.34 = (bf16[144,192]{1,0:T(8,128)(2,1)S(1)}, bf16[144,192]{1,0:T(8,128)(2,1)}, u32[]{:S(2)}) copy-start(bf16[144,192]{1,0:T(8,128)(2,1)} %param.21) | copy-start | bytes 165892
  7.2 205.8 %all-gather.6.cloned.1.call-start = ((), (), s32[]{:S(2)}) async-start(), calls=%async_computation.8 | async-start | bytes 2211840 | tf_op jit(solution)/shard_map/all_gather | solution.py:132
  7.9 213.4 %all-gather.4.cloned.1.call-start = ((), (), s32[]{:S(2)}) async-start(), calls=%async_computation.7 | async-start | bytes 2211840 | tf_op jit(solution)/shard_map/all_gather | solution.py:131
  8.7 220.6 %all-gather.8.cloned.1.call-start = ((), (), s32[]{:S(2)}) async-start(), calls=%async_computation.9 | async-start | bytes 2211840 | tf_op jit(solution)/shard_map/all_gather | solution.py:133
  9.4 514.2 %reduce-scatter.12.cloned.1.call-start = ((), (), s32[]{:S(2)}) async-start(), calls=%async_computation.12 | async-start | bytes 737280 | tf_op jit(solution)/shard_map/reduce_scatter | solution.py:237
  31.2 110.4 %copy-start.37 = (f32[576]{0:T(1024)}, f32[576]{0:T(1024)S(1)}, u32[]{:S(2)}) copy-start(f32[576]{0:T(1024)S(1)} %convert_element_type.91) | copy-start | bytes 6916
  33.1 108.5 %copy-start.35 = (f32[1536]{0:T(1024)}, f32[1536]{0:T(1024)S(1)}, u32[]{:S(2)}) copy-start(f32[1536]{0:T(1024)S(1)} %add_rsqrt_fusion.1) | copy-start | bytes 18436
  49.5 77.9 %copy-start.14 = (bf16[576,192]{1,0:T(8,128)(2,1)}, bf16[576,192]{1,0:T(8,128)(2,1)S(1)}, u32[]{:S(2)}) copy-start(bf16[576,192]{1,0:T(8,128)(2,1)S(1)} %all_gather.38) | copy-start | bytes 663556
  65.3 5.5 copy-start.23
  66.8 4.0 copy-start.31
  66.8 30.7 %copy-start.32 = (bf16[144,576]{1,0:T(8,128)(2,1)S(1)}, bf16[144,576]{1,0:T(8,128)(2,1)}, u32[]{:S(2)}) copy-start(bf16[144,576]{1,0:T(8,128)(2,1)} %param.22) | copy-start | bytes 497668
  66.8 55.9 %copy-start.40 = (f32[32]{0:T(128)S(1)}, f32[32]{0:T(128)}, u32[]{:S(2)}) copy-start(f32[32]{0:T(128)} %multiply_power_fusion) | copy-start | bytes 388
  138.2 3.3 copy-start.27
  171.6 1.9 copy-start.18
  177.2 1.2 copy-start.19
  181.9 1.9 copy-start.18
  187.6 1.2 copy-start.19
  192.3 1.9 copy-start.18
  198.0 1.2 copy-start.19
  199.2 4.3 copy-start.29
  202.9 4.1 copy-start.17
  203.6 4.1 copy-start.41
  213.0 8.4 copy-start.16
  229.3 14.9 %copy-start.44 = (bf16[576,1536]{1,0:T(8,128)(2,1)S(1)}, bf16[576,1536]{1,0:T(8,128)(2,1)}, u32[]{:S(2)}) copy-start(bf16[576,1536]{1,0:T(8,128)(2,1)} %all-gather.4.cloned.1.call-done) | copy-start | bytes 5308420
  244.2 3.0 copy-start.46
  244.2 4.6 copy-start.45
  244.2 4.6 copy-start.6
  244.2 5.8 copy-start.43
  250.1 4.0 copy-start.20
  254.1 2.9 copy-start.30
  255.2 1.7 copy-start.4
  265.1 198.0 %copy-start.36 = (f32[1536]{0:T(1024)S(1)}, f32[1536]{0:T(1024)}, u32[]{:S(2)}) copy-start(f32[1536]{0:T(1024)} %copy-done.35) | copy-start | bytes 18436
  265.1 198.0 %copy-start.38 = (f32[576]{0:T(1024)S(1)}, f32[576]{0:T(1024)}, u32[]{:S(2)}) copy-start(f32[576]{0:T(1024)} %copy-done.37) | copy-start | bytes 6916
  266.9 2.5 copy-start.8
  269.4 3.8 copy-start
  290.5 4.0 copy-start.1
  331.9 2.5 copy-start.8
  334.4 3.8 copy-start
  355.5 4.0 copy-start.1
  396.9 2.5 copy-start.8
  399.4 3.8 copy-start
  420.5 4.0 copy-start.1
  462.1 4.0 copy-start.9
  466.1 1.5 copy-start.11
  466.1 57.5 %reduce-scatter.10.cloned.1.call-start = ((), (), s32[]{:S(2)}) async-start(), calls=%async_computation.11 | async-start | bytes 737280 | tf_op jit(solution)/shard_map/reduce_scatter | solution.py:236
  467.7 1.5 copy-start.3
  470.7 74.2 %reduce-scatter.14.cloned.1.call-start = ((), (), s32[]{:S(2)}) async-start(), calls=%async_computation.13 | async-start | bytes 1843200 | tf_op jit(solution)/shard_map/reduce_scatter | solution.py:238
  476.1 104.6 %reduce-scatter.8.cloned.1.call-start = ((), (), s32[]{:S(2)}) async-start(), calls=%async_computation.10 | async-start | bytes 1843200 | tf_op jit(solution)/shard_map/reduce_scatter | solution.py:235
  482.9 4.2 copy-start.5
  493.0 155.3 %reduce-scatter.20.cloned.1.call-start = ((), (), s32[]{:S(2)}) async-start(), calls=%async_computation.16 | async-start | bytes 4423680 | tf_op jit(solution)/shard_map/reduce_scatter | solution.py:242
  500.7 216.6 %reduce-scatter.16.cloned.1.call-start = ((), (), s32[]{:S(2)}) async-start(), calls=%async_computation.14 | async-start | bytes 4423680 | tf_op jit(solution)/shard_map/reduce_scatter | solution.py:240
  508.5 277.6 %reduce-scatter.18.cloned.1.call-start = ((), (), s32[]{:S(2)}) async-start(), calls=%async_computation.15 | async-start | bytes 4423680 | tf_op jit(solution)/shard_map/reduce_scatter | solution.py:241
  516.3 352.0 %all-reduce.10.cloned.1.call-start = ((), (), s32[]{:S(2)}) async-start(), calls=%async_computation.17 | async-start | bytes 7372800 | tf_op jit(solution)/shard_map/psum | solution.py:244
  517.2 1.5 copy-start.22
  517.2 1.7 copy-start.28
  518.9 1.5 copy-start.13
  518.9 1.6 copy-start.24
  523.6 262.5 %copy-start.39 = (f32[576]{0:T(1024)S(1)}, f32[576]{0:T(1024)}, u32[]{:S(2)}) copy-start(f32[576]{0:T(1024)} %get-tuple-element.159) | copy-start | bytes 6916
  810.3 5.7 copy-start.7
  810.3 5.7 copy-start.42
  868.2 8.9 %copy-start.26 = (f32[144,1536]{1,0:T(8,128)S(1)}, f32[144,1536]{1,0:T(8,128)}, u32[]{:S(2)}) copy-start(f32[144,1536]{1,0:T(8,128)} %get-tuple-element.416) | copy-start | bytes 2654212
  868.2 9.8 %copy-start.25 = (f32[384,576]{0,1:T(8,128)S(1)}, f32[384,576]{0,1:T(8,128)}, u32[]{:S(2)}) copy-start(f32[384,576]{0,1:T(8,128)} %get-tuple-element.417) | copy-start | bytes 2654212
  (4 other events, 4.0 us)
Sparse Core Ops, SparseCore 0:
  9.6 51.8 all-gather.5
  63.1 58.6 all-gather.3
  123.4 39.5 all-gather.7
  466.2 21.3 reduce-scatter.11
  490.3 20.2 reduce-scatter.9
  512.8 32.1 reduce-scatter.13
  547.9 32.6 reduce-scatter.7
  583.0 65.2 reduce-scatter.19
  650.6 66.6 reduce-scatter.15
  719.4 66.6 reduce-scatter.17
  790.4 77.8 all-reduce.9
where the time goes:
time: 893 us; the launch traced here: 886 us
  waiting for transfers between devices  310 us (35%)
  local copies, waits for them, and re-layouts  184 us (21%)
  matrix products  171 us (19%)
  blocking collectives  122 us (14%)
  other arithmetic  80.7 us (9%)
  between operations  16 us (2%)
    dynamic_update_slice x6, local copies, waits for them, and re-layouts, shards(): lax.map(attend_block, (query_blocks, key_blocks, value_blocks, allowed))  74.1 us
    reduce_scatter x1, waiting for transfers between devices, shards(): lax.psum_scatter(gate_w_grad, 'shard', scatter_dimension=0, tiled=True)  69 us
    reduce_scatter x1, waiting for transfers between devices, shards(): lax.psum_scatter(up_w_grad, 'shard', scatter_dimension=0, tiled=True)  68.8 us
    reduce_scatter x1, waiting for transfers between devices, shards(): lax.psum_scatter(down_grad, 'shard', scatter_dimension=0, tiled=True)  67.6 us
    psum x1, waiting for transfers between devices, shards(): lax.psum((owned_grads[0], owned_grads[1], owned_grads[2], owned_grads[3],...  45.8 us
    reduce_scatter x1, waiting for transfers between devices, shards(): lax.psum_scatter(query_w_grad, 'shard', scatter_dimension=0, tiled=True)  35.7 us
    dot_general x7, matrix products, contract_rows(): lax.dot_general(former, latter, (((0,), (0,)), ((), ())), preferred_eleme...  35.4 us
    convert_element_type x3, other arithmetic, attend_back(): score_grad = (probs_all * (probs_grad - jnp.sum(probs_all * probs_grad, a...  33.7 us
  transfers between devices with their start and end apart: 11, of which 6 were waited for; matrix products, arithmetic and copies ran while one was open for 21% of the time, Pallas kernels for 0%

commit v1 on v0

v1 whole, which is shorter than its diff:
```python
import functools

import jax
import jax.numpy as jnp
from jax import lax
from jax.experimental import pallas as pl
from jax.experimental.pallas import tpu as pltpu
from jax.sharding import PartitionSpec as P

HQ = 9
KVH = 3
HD = 64
BLOCK = 512
HALF = 256
SLOT = 128
GROUPS = HQ // KVH
EPS = 1e-05
FAR = -1e30
VMEM_BYTES = 56 * 1024 * 1024

f32 = jnp.float32
bf16 = jnp.bfloat16


def dot(a, b):
    return lax.dot_general(a, b, (((1,), (0,)), ((), ())), preferred_element_type=f32)


def dot_t(a, b):
    return lax.dot_general(a, b, (((1,), (1,)), ((), ())), preferred_element_type=f32)


def slot(h):
    return pl.ds(pl.multiple_of(h * SLOT, SLOT), SLOT)


def split3(v):
    hi = v.astype(bf16).astype(f32)
    rest = v - hi
    mid = rest.astype(bf16).astype(f32)
    return hi, mid, rest - mid


def roll_half(v):
    return pltpu.roll(v, SLOT // 2, 1)


def attn_fwd(tok, cs, seg, gain, wqkv, q_out, k_out, v_out, mixed_out):
    x = tok[...].astype(f32)
    inv = lax.rsqrt(jnp.mean(x * x, axis=1, keepdims=True) + EPS)
    n = (x * inv * gain[...]).astype(bf16)
    lane = lax.broadcasted_iota(jnp.int32, (BLOCK, SLOT), 1)
    low = lane < HD
    same = (lane - 72) == seg[...]
    q_ext = jnp.where((lane >= 72) & (lane < 80) & jnp.logical_not(same), FAR, 0.0)
    k_ext = jnp.where(same | ((lane >= 64) & (lane < 67)), 1.0, 0.0)
    table = cs[...]
    for g in range(KVH):
        base = g * GROUPS * SLOT
        raw = dot(n, wqkv[:, base : base + GROUPS * SLOT])
        for j in range(GROUPS):
            r = raw[:, j * SLOT : (j + 1) * SLOT] * table
            r = (r + roll_half(r)) * (HD ** -0.5)
            q_out[:, base + j * SLOT : base + (j + 1) * SLOT] = jnp.where(low, r, q_ext).astype(bf16)
    raw = dot(n, wqkv[:, HQ * SLOT : (HQ + KVH) * SLOT])
    for g in range(KVH):
        r = raw[:, g * SLOT : (g + 1) * SLOT] * table
        r = r + roll_half(r)
        k_out[:, g * SLOT : (g + 1) * SLOT] = jnp.where(low, r, k_ext).astype(bf16)
    raw = dot(n, wqkv[:, (HQ + KVH) * SLOT :])
    for g in range(KVH):
        v_out[:, g * SLOT : (g + 1) * SLOT] = jnp.where(low, raw[:, g * SLOT : (g + 1) * SLOT], 1.0).astype(bf16)

    lane_h = lax.broadcasted_iota(jnp.int32, (HALF, SLOT), 1)
    low_h = lane_h < HD

    def group(g, carry):
        for j in range(GROUPS):
            h = g * GROUPS + j
            for i in range(2):
                rows = slice(i * HALF, (i + 1) * HALF)
                width = (i + 1) * HALF
                q = q_out[rows, slot(h)]
                s = dot_t(q, k_out[:width, slot(g)])
                seen = (
                    lax.broadcasted_iota(jnp.int32, (HALF, width), 0) + i * HALF
                    >= lax.broadcasted_iota(jnp.int32, (HALF, width), 1)
                )
                s = jnp.where(seen, s, FAR)
                m = jnp.max(s, axis=1, keepdims=True)
                e = jnp.exp(s - m).astype(bf16)
                r = dot(e, v_out[:width, slot(g)])
                total = jnp.where(low_h, roll_half(r), r)
                mixed_out[rows, slot(h)] = jnp.where(low_h, r / total, 0.0).astype(bf16)
                hi, mid, lo = split3(m + jnp.log(total))
                q = jnp.where(lane_h == 64, -hi, q.astype(f32))
                q = jnp.where(lane_h == 65, -mid, q)
                q = jnp.where(lane_h == 66, -lo, q)
                q_out[rows, slot(h)] = q.astype(bf16)
        return carry

    lax.fori_loop(0, KVH, group, 0)


def norm_back(g, x, inv, gain):
    u = g * gain
    part = inv * (u - x * (inv * inv) * jnp.mean(u * x, axis=1, keepdims=True))
    return part, jnp.sum(g * x * inv, axis=0, keepdims=True)


CHUNK = 512


def ffn(tok, mixed, cot, gain, wout, wg, wu, wd, out, mgrad, xgrad, dout, dg, du, dd, dgain, n2, n2t, cott, acc, back):
    @pl.when(pl.program_id(0) == 0)
    def _():
        dout[...] = jnp.zeros_like(dout)
        dg[...] = jnp.zeros_like(dg)
        du[...] = jnp.zeros_like(du)
        dd[...] = jnp.zeros_like(dd)
        dgain[...] = jnp.zeros_like(dgain)

    middle = tok[...].astype(f32) + dot(mixed[...], wout[...])
    inv = lax.rsqrt(jnp.mean(middle * middle, axis=1, keepdims=True) + EPS)
    normed = middle * inv * gain[...]
    n2[...] = normed.astype(bf16)
    n2t[...] = normed.T.astype(bf16)
    cott[...] = cot[...].astype(f32).T.astype(bf16)
    acc[...] = middle
    back[...] = jnp.zeros_like(back)

    def step(c, carry):
        part = pl.ds(pl.multiple_of(c * CHUNK, CHUNK), CHUNK)
        a = dot(n2[...], wg[:, part])
        b = dot(n2[...], wu[:, part])
        s = jax.nn.sigmoid(a)
        silu = a * s
        h = (silu * b).astype(bf16)
        hg = dot_t(cot[...], wd[part, :])
        ga = (hg * b * (s * (1.0 + a * (1.0 - s)))).astype(bf16)
        ub = (hg * silu).astype(bf16)
        acc[...] += dot(h, wd[part, :])
        dd[:, part] += dot(cott[...], h)
        dg[:, part] += dot(n2t[...], ga)
        du[:, part] += dot(n2t[...], ub)
        back[...] += dot_t(ga, wg[:, part]) + dot_t(ub, wu[:, part])
        return carry

    lax.fori_loop(0, wg.shape[1] // CHUNK, step, 0)
    out[...] = acc[...].astype(bf16)
    middle = tok[...].astype(f32) + dot(mixed[...], wout[...])
    inv = lax.rsqrt(jnp.mean(middle * middle, axis=1, keepdims=True) + EPS)
    part, gain_part = norm_back(back[...], middle, inv, gain[...])
    dgain[...] += gain_part
    total = cot[...].astype(f32) + part
    mgrad[...] = total
    branch = total.astype(bf16)
    xgrad[...] = dot_t(branch, wout[...]).astype(bf16)
    dout[...] += dot(mixed[...].astype(f32).T.astype(bf16), branch)


def attn_bwd(tok, cs, gain, wqkv, q_in, k_in, v_in, mixed, xgrad, mgrad, igrad, dw, dgain, dpad):
    @pl.when(pl.program_id(0) == 0)
    def _():
        dw[...] = jnp.zeros_like(dw)
        dgain[...] = jnp.zeros_like(dgain)

    lane = lax.broadcasted_iota(jnp.int32, (BLOCK, SLOT), 1)
    low = lane < HD
    table = cs[...]
    wide_seen = lax.broadcasted_iota(jnp.int32, (HALF, BLOCK), 0) <= lax.broadcasted_iota(jnp.int32, (HALF, BLOCK), 1)
    near_seen = wide_seen[:, :HALF]

    def group(g, carry):
        k = k_in[:, slot(g)]
        v = v_in[:, slot(g)]
        kt = k.astype(f32).T.astype(bf16)
        dk0 = dv0 = dk1 = dv1 = None
        for j in range(GROUPS):
            h = g * GROUPS + j
            q = q_in[:, slot(h)]
            go = xgrad[:, slot(h)].astype(f32)
            delta = jnp.sum(go * mixed[:, slot(h)].astype(f32), axis=1, keepdims=True)
            hi, mid, lo = split3(delta)
            go = jnp.where(lane == 64, -hi, go)
            go = jnp.where(lane == 65, -mid, go)
            go = jnp.where(lane == 66, -lo, go).astype(bf16)
            p0 = jnp.exp(jnp.where(wide_seen, dot_t(k[:HALF], q), FAR))
            s0 = (p0 * dot_t(v[:HALF], go)).astype(bf16)
            dv = dot(p0.astype(bf16), go)
            dk = dot(s0, q)
            dv0 = dv if dv0 is None else dv0 + dv
            dk0 = dk if dk0 is None else dk0 + dk
            p1 = jnp.exp(jnp.where(near_seen, dot_t(k[HALF:], q[HALF:]), FAR))
            s1 = (p1 * dot_t(v[HALF:], go[HALF:])).astype(bf16)
            dv = dot(p1.astype(bf16), go[HALF:])
            dk = dot(s1, q[HALF:])
            dv1 = dv if dv1 is None else dv1 + dv
            dk1 = dk if dk1 is None else dk1 + dk
            first = dot(kt[:, :HALF], s0)
            near = first[:, :HALF].T
            far = (first[:, HALF:] + dot(kt[:, HALF:], s1)).T
            dq = jnp.concatenate([near, far], axis=0) * (HD ** -0.5)
            dq = jnp.where(low, dq, 0.0)
            dpad[:, slot(h)] = ((dq + roll_half(dq)) * table).astype(bf16)
        dk = jnp.where(low, jnp.concatenate([dk0, dk1], axis=0), 0.0)
        dpad[:, slot(HQ + g)] = ((dk + roll_half(dk)) * table).astype(bf16)
        dv = jnp.where(low, jnp.concatenate([dv0, dv1], axis=0), 0.0)
        dpad[:, slot(HQ + KVH + g)] = dv.astype(bf16)
        return carry

    lax.fori_loop(0, KVH, group, 0)
    x = tok[...].astype(f32)
    inv = lax.rsqrt(jnp.mean(x * x, axis=1, keepdims=True) + EPS)
    nt = (x * inv * gain[...]).T.astype(bf16)
    dw[...] += dot(nt, dpad[...])
    part, gain_part = norm_back(dot_t(dpad[...], wqkv[...]), x, inv, gain[...])
    dgain[...] += gain_part
    igrad[...] = (mgrad[...] + part).astype(bf16)


def rows_spec(width):
    return pl.BlockSpec((BLOCK, width), lambda i: (i, 0))


def whole_spec(shape):
    return pl.BlockSpec(shape, lambda i: (0, 0), pipeline_mode=pl.Buffered(1))


def sum_spec(shape):
    return pl.BlockSpec(shape, lambda i: (0, 0))


def params():
    return pltpu.CompilerParams(vmem_limit_bytes=VMEM_BYTES, dimension_semantics=("arbitrary",))


def turned(w):
    half = HD // 2
    return jnp.concatenate([-w[..., half:], w[..., :half]], axis=-1)


def unturned(w):
    half = HD // 2
    return jnp.concatenate([w[..., half:], -w[..., :half]], axis=-1)


def tables_of(segments):
    rows = segments.shape[0]
    ids = segments.reshape(rows // BLOCK, BLOCK)
    index = jnp.arange(BLOCK, dtype=jnp.int32)
    earlier = jnp.concatenate([ids[:, :1] - 1, ids[:, :-1]], axis=1)
    starts = jnp.where(ids != earlier, index[None, :], 0)
    places = (index[None, :] - lax.cummax(starts, axis=1)).astype(f32).reshape(rows, 1)
    frequency = 100000.0 ** (jnp.arange(HD // 2, dtype=f32) * (-2.0 / HD))
    angles = places * frequency
    cosine, sine = jnp.cos(angles), jnp.sin(angles)
    return jnp.concatenate([cosine, cosine, sine, sine], axis=1)


def gather_weights(norm_attn, w_query, w_key, w_value, w_out, norm_ffn, w_gate, w_up, w_down):
    rows = norm_attn.shape[0]
    gains = jnp.concatenate(
        [norm_attn[:, None], norm_ffn[:, None], jnp.zeros((rows, SLOT - 2), bf16)], axis=1
    )
    down = w_down.reshape(rows, -1)
    packed = jnp.concatenate([w_gate, w_up, w_query, w_key, w_value, w_out, gains, down], axis=1)
    full = lax.all_gather(packed, "shard", axis=0, tiled=True)
    ff, d = w_gate.shape[1], w_query.shape[1]
    at = 2 * ff
    qk = full[:, at : at + (HQ + KVH) * HD]
    at += (HQ + KVH) * HD
    wv = full[:, at : at + KVH * HD]
    at += KVH * HD
    wout = full[:, at : at + d]
    at += d
    gain_one = full[:, at].astype(f32)[None, :]
    gain_two = full[:, at + 1].astype(f32)[None, :]
    at += SLOT
    wdown = full[:, at:].reshape(ff, d)
    return full[:, :ff], full[:, ff : 2 * ff], qk, wv, wout, gain_one, gain_two, wdown


def reduce_grads(by_columns):
    summed = lax.psum_scatter(by_columns, "shard", scatter_dimension=0, tiled=True)
    return lax.psum(summed, "dp").astype(f32)


def shards(tokens, segments, norm_attn, w_query, w_key, w_value, w_out, norm_ffn, w_gate, w_up, w_down, cotangent):
    rows, d = tokens.shape
    ff = w_gate.shape[1]
    nshard = d // norm_attn.shape[0]
    grid = (rows // BLOCK,)
    wg, wu, qk, wv, wout, gain_one, gain_two, wdown = gather_weights(
        norm_attn, w_query, w_key, w_value, w_out, norm_ffn, w_gate, w_up, w_down
    )
    qk = qk.reshape(d, HQ + KVH, HD)
    qk = jnp.concatenate([qk, turned(qk)], axis=-1).reshape(d, -1)
    wv = jnp.pad(wv.reshape(d, KVH, HD), ((0, 0), (0, 0), (0, SLOT - HD))).reshape(d, -1)
    wqkv = jnp.concatenate([qk, wv], axis=1)
    wout = jnp.pad(wout.reshape(HQ, HD, d), ((0, 0), (0, SLOT - HD), (0, 0))).reshape(HQ * SLOT, d)
    cs = tables_of(segments)
    seg = segments[:, None]
    qw, kw, allw = HQ * SLOT, KVH * SLOT, (HQ + 2 * KVH) * SLOT
    shape = jax.ShapeDtypeStruct

    q, k, v, mixed = pl.pallas_call(
        attn_fwd,
        grid=grid,
        in_specs=[rows_spec(d), rows_spec(SLOT), rows_spec(1), whole_spec((1, d)), whole_spec((d, allw))],
        out_specs=[rows_spec(qw), rows_spec(kw), rows_spec(kw), rows_spec(qw)],
        out_shape=[shape((rows, qw), bf16), shape((rows, kw), bf16), shape((rows, kw), bf16), shape((rows, qw), bf16)],
        compiler_params=params(),
        name="attn_fwd",
    )(tokens, cs, seg, gain_one, wqkv)

    output, mgrad, xgrad, dout, dg, du, dd, dgain_two = pl.pallas_call(
        ffn,
        grid=grid,
        in_specs=[
            rows_spec(d), rows_spec(qw), rows_spec(d), whole_spec((1, d)), whole_spec((qw, d)),
            whole_spec((d, ff)), whole_spec((d, ff)), whole_spec((ff, d)),
        ],
        out_specs=[
            rows_spec(d), rows_spec(d), rows_spec(qw), whole_spec((qw, d)), whole_spec((d, ff)),
            whole_spec((d, ff)), whole_spec((d, ff)), whole_spec((1, d)),
        ],
        out_shape=[
            shape((rows, d), bf16), shape((rows, d), f32), shape((rows, qw), bf16), shape((qw, d), f32),
            shape((d, ff), f32), shape((d, ff), f32), shape((d, ff), f32), shape((1, d), f32),
        ],
        scratch_shapes=[
            pltpu.VMEM((BLOCK, d), bf16), pltpu.VMEM((d, BLOCK), bf16), pltpu.VMEM((d, BLOCK), bf16),
            pltpu.VMEM((BLOCK, d), f32), pltpu.VMEM((BLOCK, d), f32),
        ],
        compiler_params=params(),
        name="ffn",
    )(tokens, mixed, cotangent, gain_two, wout, wg, wu, wdown)

    igrad, dw, dgain_one = pl.pallas_call(
        attn_bwd,
        grid=grid,
        in_specs=[
            rows_spec(d), rows_spec(SLOT), whole_spec((1, d)), whole_spec((d, allw)), rows_spec(qw),
            rows_spec(kw), rows_spec(kw), rows_spec(qw), rows_spec(qw), rows_spec(d),
        ],
        out_specs=[rows_spec(d), whole_spec((d, allw)), whole_spec((1, d))],
        out_shape=[shape((rows, d), bf16), shape((d, allw), f32), shape((1, d), f32)],
        scratch_shapes=[pltpu.VMEM((BLOCK, allw), bf16)],
        compiler_params=params(),
        name="attn_bwd",
    )(tokens, cs, gain_one, wqkv, q, k, v, mixed, xgrad, mgrad)

    dqk = dw[:, : (HQ + KVH) * SLOT].reshape(d, HQ + KVH, SLOT)
    dqk = (dqk[..., :HD] + unturned(dqk[..., HD:])).reshape(d, -1)
    dv = dw[:, (HQ + KVH) * SLOT :].reshape(d, KVH, SLOT)[..., :HD].reshape(d, -1)
    dout = dout.reshape(HQ, SLOT, d)[:, :HD].reshape(d, d)
    own_ff = ff // nshard
    dd = dd.reshape(d, nshard, own_ff).transpose(1, 0, 2).reshape(nshard * own_ff, d)
    dd = dd.reshape(d, ff)
    first = jnp.concatenate([dg.astype(bf16), du.astype(bf16), dd.astype(bf16)], axis=1)
    gains = jnp.concatenate([dgain_one.T, dgain_two.T, jnp.zeros((d, SLOT - 2), f32)], axis=1)
    second = jnp.concatenate([dqk, dv, dout, gains], axis=1).astype(bf16)
    first = reduce_grads(first)
    second = reduce_grads(second)
    own_d = d // nshard
    down = first[:, 2 * ff :].reshape(d, own_ff).T
    nq, nk = HQ * HD, KVH * HD
    at = nq + 2 * nk
    return (
        output,
        igrad,
        second[:, at + d],
        second[:, :nq],
        second[:, nq : nq + nk],
        second[:, nq + nk : at],
        second[:, at : at + d],
        second[:, at + d + 1],
        first[:, :ff],
        first[:, ff : 2 * ff],
        down,
    )


def solution(mesh):
    rows = P(("dp", "shard"), None)
    weight, gain = P("shard", None), P("shard")
    in_specs = (
        rows, P(("dp", "shard")), gain, weight, weight, weight, weight, gain, weight, weight, weight, rows
    )
    out_specs = (rows, rows, gain, weight, weight, weight, weight, gain, weight, weight, weight)
    return jax.shard_map(shards, mesh=mesh, in_specs=in_specs, out_specs=out_specs, check_vma=False)
```

time: 893 us -> 537 us (0.60)
  matrix products: 171 us -> 0 us
  Pallas kernels: 0 us -> 129 us
  blocking collectives: 122 us -> 0 us
  local copies, waits for them, and re-layouts: 184 us -> 67.4 us
  other arithmetic: 80.7 us -> 23.7 us
    dot_general x42 -> x0, matrix products: 171 us -> none  [the longest x7 35.4 us: contract_rows(): lax.dot_general(former, latter, (((0,), (0,)), ((), ())), preferred_eleme...]
    reduce_scatter x7 -> x1, waiting for transfers between devices: 262 us -> 94.1 us  [reduce_grads(): lax.psum_scatter(by_columns, 'shard', scatter_dimension=0, tiled=True)]
    pallas_call x0 -> x3, Pallas kernels: none -> 129 us  [the longest x1 59.2 us: shards(): pl.pallas_call(ffn, grid=grid, in_specs=[rows_spec(d), rows_spec(qw), row...]
    all_gather x3 -> x1, waiting for transfers between devices: 0.02 us -> 118 us  [gather_weights(): full = lax.all_gather(packed, 'shard', axis=0, tiled=True)]
    dynamic_update_slice x12 -> x0, local copies, waits for them, and re-layouts: 101 us -> none  [the longest x6 74.1 us: shards(): lax.map(attend_block, (query_blocks, key_blocks, value_blocks, allowed))]
    all_gather x4 -> x0, blocking collectives: 84.1 us -> none  [the longest x1 26.7 us: shards(): lax.all_gather(w_query, 'shard', axis=0, tiled=True)]
    convert_element_type x13 -> x5, other arithmetic: 51.4 us -> 6.07 us  [the longest x1 2.41 us: shards(): dg.astype(bf16)]
    unnamed x11 -> x5, waiting for transfers between devices: 2.19 us -> 29.1 us
  transfers between devices with their start and end apart: 11 -> 4, of which waited for: 6 -> 4; matrix products, arithmetic and copies ran while one was open for 21% -> 6% of each run, Pallas kernels for 0% -> 0%
where the time goes in v1:
time: 537 us; the launch traced here: 536 us
  waiting for transfers between devices  302 us (56%)
  Pallas kernels  129 us (24%)
  local copies, waits for them, and re-layouts  67.4 us (13%)
  other arithmetic  23.7 us (4%)
  between operations  14.2 us (3%)
    all_gather x1, waiting for transfers between devices, gather_weights(): full = lax.all_gather(packed, 'shard', axis=0, tiled=True)  118 us
    reduce_scatter x1, waiting for transfers between devices, reduce_grads(): lax.psum_scatter(by_columns, 'shard', scatter_dimension=0, tiled=True)  94.1 us
    psum x1, waiting for transfers between devices, reduce_grads(): return lax.psum(summed, 'dp').astype(f32)  60.8 us
    pallas_call x1, Pallas kernels, shards(): pl.pallas_call(ffn, grid=grid, in_specs=[rows_spec(d), rows_spec(qw), row...  59.2 us
    pallas_call x1, Pallas kernels, shards(): pl.pallas_call(attn_bwd, grid=grid, in_specs=[rows_spec(d), rows_spec(SLO...  36.8 us
    pallas_call x1, Pallas kernels, shards(): pl.pallas_call(attn_fwd, grid=grid, in_specs=[rows_spec(d), rows_spec(SLO...  33.1 us
    unnamed x5, waiting for transfers between devices  29.1 us
    unnamed x43, local copies, waits for them, and re-layouts  21.4 us
  transfers between devices with their start and end apart: 4, of which 4 were waited for; matrix products, arithmetic and copies ran while one was open for 6% of the time, Pallas kernels for 0%

profile of v1, /device:TPU:0, one launch (start us, length us, event | category | flops | bytes accessed | tf_op | source)
XLA Modules:
  0.0 536.5 jit_solution(4893572988667378435)
XLA Ops:
  7.3 1.4 copy.98
  8.7 0.7 reshape.150
  9.4 0.7 broadcast_in_dim.37
  10.1 0.7 broadcast_in_dim.38
  11.0 2.8 concatenate.30
  13.8 0.6 reshape.147
  14.4 1.1 broadcast_in_dim.36.seg
  15.7 0.8 compare_select_fusion
  16.5 0.9 reduce-window.6
  17.6 0.8 reduce-window.9
  18.4 0.8 broadcast_maximum_fusion
  19.2 0.6 sub.25
  19.8 0.7 sub.26
  20.5 2.3 copy.107.tok
  22.7 2.3 copy.108.cot
  25.0 2.8 multiply_cosine_fusion
  27.8 1.6 pad_maximum_fusion.3.cs
  29.4 117.9 %all-gather.2.cloned.1.call-done = bf16[576,6272]{1,0:T(8,128)(2,1)} async-done(((bf16[144,6272]{1,0:T(8,128)(2,1)}), bf16[576,6272]{1,0:T(8,128)(2,1)}) %all-gather.2.cloned.1.call-update) | async-done | bytes 7225360 | tf_op jit(solution)/shard_map/all_gather | solution.py:268
  147.2 1.2 slice-done
  148.4 0.6 copy.101
  149.4 2.2 copy.103
  151.8 0.2 copy.104
  152.1 1.2 convert_reduce_fusion
  153.3 0.6 reshape.165.gain
  153.9 4.7 fusion.1
  158.6 3.9 reshape.157.wd
  162.5 0.6 reshape.166.gain
  163.0 1.5 slice.135
  164.6 1.3 pad.9
  165.8 1.5 pad_maximum_fusion.1.wqkv
  167.4 33.1 %attn_fwd.1 = (bf16[1536,1152]{1,0:T(8,128)(2,1)}, bf16[1536,384]{1,0:T(8,128)(2,1)}, bf16[1536,384]{1,0:T(8,128)(2,1)}, bf16[1536,1152]{1,0:T(8,128)(2,1)}) custom-call(bf16[1536,576]{1,0:T(8,128)(2,1)} %copy.107.tok, f32[1536,128]{1,0:T(8,128)} %pad_maximum_fusion.3.cs, s32[1536,1]{1,0:T(8,128)} %broadcast_in_dim.36.seg, f32[1,576]{1,0:T(1,128)} %reshape.165.gain, ...), custom_call_target="tpu_custom_call" | custom-call | tf_op jit(solution)/shard_map/attn_fwd/pallas_call | solution.py:307
  200.5 59.2 %ffn.1 = (bf16[1536,576]{1,0:T(8,128)(2,1)}, f32[1536,576]{1,0:T(8,128)}, bf16[1536,1152]{1,0:T(8,128)(2,1)}, f32[1152,576]{1,0:T(8,128)}, f32[576,1536]{1,0:T(8...) custom-call(bf16[1536,576]{1,0:T(8,128)(2,1)} %copy.107.tok, ...), custom_call_target="tpu_custom_call" | custom-call | tf_op jit(solution)/shard_map/ffn/pallas_call | solution.py:317
  259.7 36.8 %attn_bwd.1 = (bf16[1536,576]{1,0:T(8,128)(2,1)}, f32[576,1920]{1,0:T(8,128)}, f32[1,576]{1,0:T(1,128)}) custom-call(bf16[1536,576]{1,0:T(8,128)(2,1)} %copy.107.tok, f32[1536,128]{1,0:T(8,128)} %pad_maximum_fusion.3.cs, f32[1,576]{1,0:T(1,128)} %reshape.165.gain, bf16[576,1920]{1,0:T(8,128)(2,1)} %pad_maximum_fusion.1.wqkv, ...), custom_call_target="tpu_custom_call" | custom-call | tf_op jit(solution)/shard_map/attn_bwd/pallas_call | solution.py:340
  296.5 2.2 slice.110
  298.7 2.0 slice.164
  300.7 3.1 copy.110
  303.8 1.7 fusion.2
  305.5 0.3 copy.111
  305.9 2.0 convert.31
  307.9 1.2 copy.112
  309.1 1.8 fusion
  310.9 3.9 concatenate.34
  314.8 2.8 copy.120
  317.6 2.2 convert_element_type.70
  319.8 0.5 convert_element_type.71
  320.5 1.1 convert_element_type.73
  321.7 2.4 convert_element_type.68
  324.1 0.7 copy-done.2
  325.0 2.7 pad_maximum_fusion
  327.8 29.1 %reduce-scatter.7.cloned.1.call-done = bf16[144,1664]{1,0:T(8,128)(2,1)} async-done(((bf16[576,1664]{1,0:T(8,128)(2,1)}), bf16[144,1664]{1,0:T(8,128)(2,1)}) %reduce-scatter.7.cloned.1.call-update) | async-done | bytes 479248
  356.9 2.2 copy.121
  359.1 94.1 %reduce-scatter.5.cloned.1.call-done = bf16[144,4608]{1,0:T(8,128)(2,1)} async-done(((bf16[576,4608]{1,0:T(8,128)(2,1)}), bf16[144,4608]{1,0:T(8,128)(2,1)}) %reduce-scatter.5.cloned.1.call-update) | async-done | bytes 1327120 | tf_op jit(solution)/shard_map/reduce_scatter | solution.py:285
  453.3 4.0 copy.115
  457.3 2.2 copy.114
  459.5 60.8 %all-reduce.5.cloned.1.call-done = (bf16[144,1664]{0,1:T(8,128)(2,1)}, bf16[144,4608]{1,0:T(8,128)(2,1)}) async-done(((bf16[144,1664]{0,1:T(8,128)(2,1)}, bf16[144,4608]{1,0:T(8,128)(2,1)}), (bf16[144,1664]{0,1:T(8,128)(2,1)}, bf16[144,4608]{1,0:T(8,128)(2,1)})) %all-reduce.5.cloned.1.call-update) | async-done | bytes 1806352 | tf_op jit(solution)/shard_map/psum | solution.py:286
  520.3 1.2 fusion.5
  521.5 1.0 fusion.6
  522.5 1.3 fusion.4
  523.8 1.5 fusion.3
  525.4 1.2 reshape.164
  526.5 0.9 copy.116
  527.5 0.9 copy.119
  528.4 0.8 copy.117
  529.2 0.8 copy.118
  (63 shorter events, 1.7 us)
Async XLA Ops:
  7.2 3.7 copy-start.9
  7.2 3.7 copy-start.12
  7.2 3.7 copy-start.13
  7.2 3.7 copy-start.10
  7.2 3.7 copy-start.7
  7.2 3.7 copy-start.8
  7.2 140.0 %all-gather.2.cloned.1.call-start = ((), (), s32[]{:S(2)}) async-start(), calls=%async_computation.2 | async-start | bytes 9031680 | tf_op jit(solution)/shard_map/all_gather | solution.py:268
  10.9 2.9 copy-start.11
  13.7 6.7 %copy-start.4 = (bf16[1536,576]{0,1:T(8,128)(2,1)S(1)}, bf16[1536,576]{0,1:T(8,128)(2,1)}, u32[]{:S(2)}) copy-start(bf16[1536,576]{0,1:T(8,128)(2,1)} %param.12) | copy-start | bytes 5308420
  13.8 343.1 %reduce-scatter.7.cloned.1.call-start = ((), (), s32[]{:S(2)}) async-start(), calls=%async_computation.4 | async-start | bytes 2396160
  15.6 7.1 %copy-start.5 = (bf16[1536,576]{0,1:T(8,128)(2,1)S(1)}, bf16[1536,576]{0,1:T(8,128)(2,1)}, u32[]{:S(2)}) copy-start(bf16[1536,576]{0,1:T(8,128)(2,1)} %param.23) | copy-start | bytes 5308420
  147.2 1.2 slice-start
  149.4 2.2 slice-start.1
  162.5 3.4 copy-start
  303.8 1.7 copy-start.6
  303.8 2.0 copy-start.15
  307.9 1.3 copy-start.14
  317.6 135.6 %reduce-scatter.5.cloned.1.call-start = ((), (), s32[]{:S(2)}) async-start(), calls=%async_computation.3 | async-start | bytes 6635520 | tf_op jit(solution)/shard_map/reduce_scatter | solution.py:285
  321.7 3.2 copy-start.2
  327.7 192.6 %all-reduce.5.cloned.1.call-start = ((), (), s32[]{:S(2)}) async-start(), calls=%async_computation.5 | async-start | bytes 4358144 | tf_op jit(solution)/shard_map/psum | solution.py:286
  453.2 4.0 copy-start.3
  520.3 3.5 copy-start.1
Sparse Core Ops, SparseCore 0:
  13.9 133.3 all-gather.1
  317.7 39.0 reduce-scatter.6
  359.2 94.0 reduce-scatter.4
  457.4 62.8 all-reduce.4
